TPU v7x, 512 devices: a whole 4x4x16 slice. The times are simulated.
512 devices in a mesh: ctx: 64 (over z, x), head: 8 (over y, core).
Axes of the slice: x: 4, y: 4, z: 16, core: 2. Of those that a mesh axis runs over, the one named last changes fastest.
Arguments:
- queries: float32 [32768, 2048], P('ctx', 'head'), may hold values from -1024 to 1024
- keys: float32 [32768, 128], P('ctx'), may hold values from -1024 to 1024
- values: float32 [32768, 128], P('ctx'), may hold values from -6 to 6
- cotangent: float32 [32768, 2048], P('ctx', 'head'), may hold values from -384 to 384
- source_ids: int32 [32768], P('ctx'), may hold values from 0 to 63
- source_weights: float32 [64], replicated, may hold values from 0.25 to 4
- q_feature: float32 [16, 128, 128], P('head'), may hold values from -4 to 4
- k_feature: float32 [128, 128], replicated, may hold values from -4 to 4
Outputs:
- grad_queries: float32 [32768, 2048], P('ctx', 'head')
- grad_keys: float32 [32768, 128], P(('ctx', 'head'))
- grad_values: float32 [32768, 128], P(('ctx', 'head'))
- grad_q_feature: float32 [16, 128, 128], P('head')
- grad_k_feature: float32 [128, 128], replicated
All inputs are finite; a program needn't handle non-finite values.
Results may differ from a plain program's by a relative error of at most 0.0015.
Values sent between devices are 32-bit elements; how exact they have to be, the bound alone decides.
A program may use at most 64 MiB of HBM per device.

v0:
```python
import jax
import jax.numpy as jnp
from jax import lax
from jax.sharding import PartitionSpec as P


def entering(value, axis, join, neutral, backward):
    count, mine = (lax.axis_size(axis), lax.axis_index(axis))
    pieces = jax.tree.map(lambda part: lax.all_gather(part, axis), value)
    if backward:
        pieces = jax.tree.map(lambda part: part[::-1], pieces)
        mine = count - 1 - mine
    total = jax.tree.map(
        lambda part, zero: jnp.full_like(part, 0) + jnp.asarray(zero, part.dtype), value, neutral
    )

    def turn(position, total):
        longer = join(total, jax.tree.map(lambda part: part[position], pieces))
        return jax.tree.map(lambda new, old: jnp.where(position < mine, new, old), longer, total)

    return lax.fori_loop(0, count - 1, turn, total)


def matmul(left, right):
    return jnp.dot(left, right, precision=lax.Precision.HIGHEST, preferred_element_type=jnp.float32)


def product(form, left, right):
    return jnp.einsum(
        form, left, right, precision=lax.Precision.HIGHEST, preferred_element_type=jnp.float32
    )


def feature_map(inputs, weight):
    logits = matmul(inputs, weight)
    upper = jax.nn.softmax(logits, axis=-1)
    lower = jax.nn.softmax(-logits, axis=-1)
    return (jnp.concatenate([upper, lower], axis=-1), upper, lower)


def feature_back(inputs, weight, upper, lower, grad_feat):
    half = upper.shape[-1]
    grad_upper = grad_feat[:, :half]
    grad_lower = grad_feat[:, half:]
    grad_logits = upper * (grad_upper - jnp.sum(upper * grad_upper, axis=-1, keepdims=True))
    grad_logits = grad_logits - lower * (
        grad_lower - jnp.sum(lower * grad_lower, axis=-1, keepdims=True)
    )
    return (matmul(grad_logits, weight.T), matmul(inputs.T, grad_logits))


def causal_mask(count):
    row_index = lax.broadcasted_iota(jnp.int32, (count, count), 0)
    col_index = lax.broadcasted_iota(jnp.int32, (count, count), 1)
    return (row_index >= col_index).astype(jnp.float32)


def add_pair(earlier, later):
    return (earlier[0] + later[0], earlier[1] + later[1])


def block_terms(query_c, key_c, value_c, scaled_c, prefix, prefix_tot):
    lower_mask = causal_mask(query_c.shape[1])
    scores = product("ncf,ndf->ncd", query_c, key_c) * lower_mask
    numerator = product("ncd,nde->nce", scores, value_c) + product("ncf,nfe->nce", query_c, prefix)
    normalizer = jnp.sum(scores, axis=2) + product("ncf,nf->nc", query_c, prefix_tot)
    output = numerator / normalizer[..., None]
    grad_numer = scaled_c / normalizer[..., None]
    grad_norm = -jnp.sum(scaled_c * output, axis=2) / normalizer
    grad_scores = (product("nce,nde->ncd", grad_numer, value_c) + grad_norm[..., None]) * lower_mask
    grad_query = (
        product("ncd,ndf->ncf", grad_scores, key_c)
        + product("nce,nfe->ncf", grad_numer, prefix)
        + grad_norm[..., None] * prefix_tot[:, None, :]
    )
    grad_key = product("ncd,ncf->ndf", grad_scores, query_c)
    grad_value = product("ncd,nce->nde", scores, grad_numer)
    carried = product("ncf,nce->nfe", query_c, grad_numer)
    carried_totals = product("nc,ncf->nf", grad_norm, query_c)
    return (grad_query, grad_key, grad_value, carried, carried_totals)


def on_device(queries, keys, values, cotangent, source_ids, source_weights, q_feature, k_feature):
    head_count = q_feature.shape[0]
    width = q_feature.shape[1]
    features = 2 * q_feature.shape[2]
    rows = queries.shape[0]
    piece = min(128, rows)
    pieces = rows // piece
    source_index = lax.broadcasted_iota(jnp.int32, (1, source_weights.shape[0]), 1)
    lookup = (source_ids[:, None] == source_index).astype(jnp.float32)
    weight = jnp.sum(lookup * source_weights[None, :], axis=1)
    key_feat, key_upper, key_lower = feature_map(keys, k_feature)
    key_c = key_feat.reshape(pieces, piece, features)
    value_c = values.reshape(pieces, piece, width)
    piece_state = product("ncf,nce->nfe", key_c, value_c)
    piece_tot = jnp.sum(key_c, axis=1)
    whole_local = (jnp.sum(piece_state, axis=0), jnp.sum(piece_tot, axis=0))
    whole_zero = (jnp.zeros((features, width), jnp.float32), jnp.zeros((features,), jnp.float32))
    earlier, earlier_totals = entering(
        (whole_local[0], whole_local[1]), "ctx", add_pair, whole_zero, False
    )
    prefix = jnp.cumsum(piece_state, axis=0) - piece_state + earlier[None]
    prefix_tot = jnp.cumsum(piece_tot, axis=0) - piece_tot + earlier_totals[None]
    grad_keyfeat = jnp.zeros(key_feat.shape, jnp.float32)
    grad_vals = jnp.zeros(values.shape, jnp.float32)
    piece_carried = jnp.zeros((pieces, features, width), jnp.float32)
    piece_carried_tot = jnp.zeros((pieces, features), jnp.float32)
    query_grads = []
    weight_grads = []
    for head in range(head_count):
        query_head = queries[:, head * width : (head + 1) * width]
        query_feat, query_upper, query_lower = feature_map(query_head, q_feature[head])
        scaled = cotangent[:, head * width : (head + 1) * width] * weight[:, None]
        grad_query, grad_key, grad_value, carried, carried_totals = block_terms(
            query_feat.reshape(pieces, piece, features),
            key_c,
            value_c,
            scaled.reshape(pieces, piece, width),
            prefix,
            prefix_tot,
        )
        grad_head, grad_weight = feature_back(
            query_head,
            q_feature[head],
            query_upper,
            query_lower,
            grad_query.reshape(rows, features),
        )
        query_grads.append(grad_head)
        weight_grads.append(grad_weight)
        grad_keyfeat = grad_keyfeat + grad_key.reshape(rows, features)
        grad_vals = grad_vals + grad_value.reshape(rows, width)
        piece_carried = piece_carried + carried
        piece_carried_tot = piece_carried_tot + carried_totals
    carried_all = jnp.sum(piece_carried, axis=0)
    carried_tot = jnp.sum(piece_carried_tot, axis=0)
    inner_later = carried_all[None] - jnp.cumsum(piece_carried, axis=0)
    inner_tot = carried_tot[None] - jnp.cumsum(piece_carried_tot, axis=0)
    grad_keyfeat = grad_keyfeat + (
        product("nce,nfe->ncf", value_c, inner_later) + inner_tot[:, None, :]
    ).reshape(rows, features)
    grad_vals = grad_vals + product("ncf,nfe->nce", key_c, inner_later).reshape(rows, width)
    later, later_tot = entering((carried_all, carried_tot), "ctx", add_pair, whole_zero, True)
    grad_keyfeat = grad_keyfeat + matmul(values, later.T) + later_tot[None, :]
    grad_vals = grad_vals + matmul(key_feat, later)
    grad_key_part, grad_kweight = feature_back(keys, k_feature, key_upper, key_lower, grad_keyfeat)
    grad_keys, grad_values = (
        lax.psum_scatter(grad_key_part, "head", scatter_dimension=0, tiled=True),
        lax.psum_scatter(grad_vals, "head", scatter_dimension=0, tiled=True),
    )
    grad_qweight = lax.psum(jnp.stack(weight_grads, axis=0), "ctx")
    grad_kweight = lax.psum(grad_kweight, ("ctx", "head"))
    return (
        jnp.concatenate(query_grads, axis=1),
        grad_keys,
        grad_values,
        grad_qweight,
        grad_kweight,
    )


def solution(mesh):
    placed = (
        P("ctx", "head"),
        P("ctx", None),
        P("ctx", None),
        P("ctx", "head"),
        P("ctx"),
        P(),
        P("head", None, None),
        P(),
    )
    return jax.shard_map(
        on_device,
        mesh=mesh,
        in_specs=placed,
        out_specs=(
            P("ctx", "head"),
            P(("ctx", "head"), None),
            P(("ctx", "head"), None),
            P("head", None, None),
            P(),
        ),
        check_vma=False,
    )
```

profile of v0, /device:TPU:2, one launch (start us, length us, event | category | flops | bytes accessed | tf_op | source)
XLA Modules:
  0.0 1215.9 jit_solution(13639607046449780209)
XLA Ops:
  9.8 2.1 fusion.103
  14.9 87.9 %all-gather.4 = f32[64,1,256]{2,1,0:T(1,128)S(1)} all-gather(f32[1,1,256]{2,1,0:T(1,128)S(1)} %bitcast.226), channel_id=3, replica_groups=mesh['ctx'=64,'head'=8] {'ctx'}, dimensions={0}, use_global_device_ids=true | all-gather | bytes 66560 | tf_op jit(solution)/shard_map/all_gather | solution.py:9
  106.6 1.8 fusion.102
  108.4 1.8 fusion.104
  110.2 62.4 %all-gather.9.cloned.1.call-done = f32[16384,128]{1,0:T(8,128)} async-done(((f32[256,128]{1,0:T(8,128)}), f32[16384,128]{1,0:T(8,128)}) %all-gather.9.cloned.1.call-update) | async-done | bytes 8388624 | tf_op jit(solution)/shard_map/all_gather | solution.py:9
  172.6 106.3 %while.32 = (s32[]{:T(128)}, f32[256,128]{1,0:T(8,128)S(1)}, f32[256]{0:T(256)S(1)}, s32[]{:T(128)}, f32[64,256,128]{2,1,0:T(8,128)}, /*index=5*/f32[64,256]{1,0:T(8,128)}, s32[]{:T(128)}, s32[]{:T(128)}) while((s32[]{:T(128)}, f32[256,128]{1,0:T(8,128)S(1)}, f32[256]{0:T(256)S(1)}, s32[]{:T(128)}, f32[64,256,128]{2,1,0:T(8,128)}, ...), condition=%wide.region_15.16_spmd.clone, body=%wide.region_14.15_spmd.clone.sunk | while | flops 99076 | bytes 398459 | solution.py:21
  280.5 2.1 fusion.105
  287.9 1.6 fusion.15
  290.7 80.2 %all-gather.5 = f32[64,1,256]{2,1,0:T(1,128)S(1)} all-gather(f32[1,1,256]{2,1,0:T(1,128)S(1)} %bitcast.225), channel_id=5, replica_groups=mesh['ctx'=64,'head'=8] {'ctx'}, dimensions={0}, use_global_device_ids=true | all-gather | bytes 66560 | tf_op jit(solution)/shard_map/all_gather | solution.py:9
  374.8 1.8 copy.214
  376.6 1.8 copy.215
  390.7 2.0 copy.209
  392.7 1.8 copy.213
  402.3 1.7 fusion.93
  405.1 1.6 fusion.7
  406.8 27.8 %all-gather.11.cloned.1.call-done = f32[16384,128]{1,0:T(8,128)} async-done(((f32[256,128]{1,0:T(8,128)}), f32[16384,128]{1,0:T(8,128)}) %all-gather.11.cloned.1.call-update) | async-done | bytes 8388624 | tf_op jit(solution)/shard_map/all_gather | solution.py:9
  434.6 7.7 rev.6
  442.2 106.4 %while.33 = (s32[]{:T(128)}, f32[256,128]{1,0:T(8,128)S(1)}, f32[256]{0:T(256)S(1)}, s32[]{:T(128)}, f32[64,256,128]{2,1,0:T(8,128)}, /*index=5*/f32[64,256]{1,0:T(8,128)}, s32[]{:T(128)}, s32[]{:T(128)}) while((s32[]{:T(128)}, f32[256,128]{1,0:T(8,128)S(1)}, f32[256]{0:T(256)S(1)}, s32[]{:T(128)}, f32[64,256,128]{2,1,0:T(8,128)}, ...), condition=%wide.region_33.34_spmd.clone, body=%wide.region_32.33_spmd.clone.sunk | while | flops 99076 | bytes 398459 | solution.py:21
  550.8 1.7 convolution_add_fusion.5
  555.7 138.0 %all-reduce.3.cloned.1.call-done = f32[2,128,128]{1,2,0:T(8,128)} async-done(((f32[2,128,128]{1,2,0:T(8,128)}), f32[2,128,128]{1,2,0:T(8,128)}) %all-reduce.3.cloned.1.call-update) | async-done | bytes 131088 | tf_op jit(solution)/shard_map/psum | solution.py:152
  693.8 1.7 copy.181
  695.4 440.1 %all-reduce.5.cloned.1.call-done = f32[128,128]{0,1:T(8,128)} async-done(((f32[128,128]{0,1:T(8,128)}), f32[128,128]{0,1:T(8,128)}) %all-reduce.5.cloned.1.call-update) | async-done | bytes 65552 | tf_op jit(solution)/shard_map/psum | solution.py:153
  1137.1 31.7 %reduce-scatter.5.cloned.1.call-done = f32[64,128]{1,0:T(8,128)} async-done(((f32[512,128]{1,0:T(8,128)}), f32[64,128]{1,0:T(8,128)}) %reduce-scatter.5.cloned.1.call-update) | async-done | bytes 32784 | tf_op jit(solution)/shard_map/reduce_scatter | solution.py:150
  1168.8 40.2 %reduce-scatter.3.cloned.1.call-done = f32[64,128]{1,0:T(8,128)} async-done(((f32[512,128]{1,0:T(8,128)}), f32[64,128]{1,0:T(8,128)}) %reduce-scatter.3.cloned.1.call-update) | async-done | bytes 32784 | tf_op jit(solution)/shard_map/reduce_scatter | solution.py:149
  (497 shorter events, 258.7 us)
Async XLA Ops:
  7.2 2.6 copy-start
  7.2 98.1 %copy-start.12 = (f32[2,128,128]{2,1,0:T(8,128)S(1)}, f32[2,128,128]{2,1,0:T(8,128)}, u32[]{:S(2)}) copy-start(f32[2,128,128]{2,1,0:T(8,128)} %param.18) | copy-start | bytes 393220
  7.2 98.1 %copy-start.4 = (f32[512,256]{1,0:T(8,128)S(1)}, f32[512,256]{1,0:T(8,128)}, u32[]{:S(2)}) copy-start(f32[512,256]{1,0:T(8,128)} %param.12) | copy-start | bytes 1572868
  7.2 165.4 %all-gather.9.cloned.1.call-start = ((), (), s32[]{:S(2)}) async-start(), calls=%async_computation.6 | async-start | bytes 8519680 | tf_op jit(solution)/shard_map/all_gather | solution.py:9
  11.9 422.7 %all-gather.11.cloned.1.call-start = ((), (), s32[]{:S(2)}) async-start(), calls=%async_computation.7 | async-start | bytes 8519680 | tf_op jit(solution)/shard_map/all_gather | solution.py:9
  105.1 174.8 %copy-start.8 = (f32[4,128,128]{1,2,0:T(8,128)S(1)}, f32[4,128,128]{1,2,0:T(8,128)}, u32[]{:S(2)}) copy-start(f32[4,128,128]{1,2,0:T(8,128)} %copy.142) | copy-start | bytes 786436
  105.3 173.6 %copy-start.10 = (f32[128,128]{0,1:T(8,128)}, f32[128,128]{0,1:T(8,128)S(1)}, u32[]{:S(2)}) copy-start(f32[128,128]{0,1:T(8,128)S(1)} %fusion.88) | copy-start | bytes 196612
  279.0 92.5 %copy-start.11 = (f32[128,128]{0,1:T(8,128)S(1)}, f32[128,128]{0,1:T(8,128)}, u32[]{:S(2)}) copy-start(f32[128,128]{0,1:T(8,128)} %copy-done.10) | copy-start | bytes 196612
  282.6 411.2 %all-reduce.3.cloned.1.call-start = ((), (), s32[]{:S(2)}) async-start(), calls=%async_computation.4 | async-start | bytes 262144 | tf_op jit(solution)/shard_map/psum | solution.py:152
  290.6 90.5 %copy-start.15 = (f32[256]{0:T(256)}, f32[256]{0:T(256)S(1)}, u32[]{:S(2)}) copy-start(f32[256]{0:T(256)S(1)} %get-tuple-element.329) | copy-start | bytes 3076
  372.0 0.7 copy-start.6
  379.8 0.7 copy-start.7
  382.8 11.8 copy-start.3
  396.6 3.7 copy-start.1
  406.7 728.8 %all-reduce.5.cloned.1.call-start = ((), (), s32[]{:S(2)}) async-start(), calls=%async_computation.5 | async-start | bytes 131072 | tf_op jit(solution)/shard_map/psum | solution.py:153
  434.6 114.1 %copy-start.5 = (f32[512,256]{0,1:T(8,128)S(1)}, f32[512,256]{0,1:T(8,128)}, u32[]{:S(2)}) copy-start(f32[512,256]{0,1:T(8,128)} %copy.209) | copy-start | bytes 1572868
  434.6 114.9 %copy-start.9 = (f32[512,128]{1,0:T(8,128)S(1)}, f32[512,128]{1,0:T(8,128)}, u32[]{:S(2)}) copy-start(f32[512,128]{1,0:T(8,128)} %param.13) | copy-start | bytes 786436
  434.6 118.0 %copy-start.14 = (f32[128,128]{1,0:T(8,128)S(1)}, f32[128,128]{1,0:T(8,128)}, u32[]{:S(2)}) copy-start(f32[128,128]{1,0:T(8,128)} %param.19) | copy-start | bytes 196612
  442.2 111.6 %copy-start.2 = (f32[512,128]{0,1:T(8,128)S(1)}, f32[512,128]{0,1:T(8,128)}, u32[]{:S(2)}) copy-start(f32[512,128]{0,1:T(8,128)} %copy-done.1) | copy-start | bytes 786436
  442.2 111.6 %copy-start.13 = (f32[2,128,128]{2,1,0:T(8,128)S(1)}, f32[2,128,128]{2,1,0:T(8,128)}, u32[]{:S(2)}) copy-start(f32[2,128,128]{2,1,0:T(8,128)} %param.18) | copy-start | bytes 393220
  550.5 618.3 %reduce-scatter.5.cloned.1.call-start = ((), (), s32[]{:S(2)}) async-start(), calls=%async_computation.3 | async-start | bytes 294912 | tf_op jit(solution)/shard_map/reduce_scatter | solution.py:150
  552.5 656.5 %reduce-scatter.3.cloned.1.call-start = ((), (), s32[]{:S(2)}) async-start(), calls=%async_computation.2 | async-start | bytes 294912 | tf_op jit(solution)/shard_map/reduce_scatter | solution.py:149
Sparse Core Ops, SparseCore 0:
  12.0 160.5 all-gather.8
  282.7 151.7 all-gather.10
  438.0 255.7 all-reduce.2
  699.7 435.8 all-reduce.4
  1139.0 29.7 reduce-scatter.4
  1172.0 36.9 reduce-scatter.2
where the time goes:
time: 1220 us
  waiting for transfers between devices  740 us (61%)
  blocking collectives  168 us (14%)
  other arithmetic  133 us (11%)
  local copies, waits for them, and re-layouts  116 us (10%)
  matrix products  40.1 us (3%)
  between operations  14.6 us (1%)
    psum x1, waiting for transfers between devices, on_device(): grad_kweight = lax.psum(grad_kweight, ('ctx', 'head'))  440 us
    all_gather x2, blocking collectives, entering(): pieces = jax.tree.map(lambda part: lax.all_gather(part, axis), value)  168 us
    psum x1, waiting for transfers between devices, on_device(): grad_qweight = lax.psum(jnp.stack(weight_grads, axis=0), 'ctx')  138 us
    select_n x252, other arithmetic, turn(): jnp.where(position < mine, new, old)  121 us
    all_gather x2, waiting for transfers between devices, entering(): pieces = jax.tree.map(lambda part: lax.all_gather(part, axis), value)  90.2 us
    dynamic_slice x126, local copies, waits for them, and re-layouts, turn(): longer = join(total, jax.tree.map(lambda part: part[position], pieces))  89 us
    reduce_scatter x1, waiting for transfers between devices, on_device(): lax.psum_scatter(grad_key_part, 'head', scatter_dimension=0, tiled=True)  40.2 us
    reduce_scatter x1, waiting for transfers between devices, on_device(): lax.psum_scatter(grad_vals, 'head', scatter_dimension=0, tiled=True)  31.7 us
  transfers between devices with their start and end apart: 6, of which 6 were waited for; matrix products, arithmetic and copies ran while one was open for 14% of the time, Pallas kernels for 0%

commit v1 on v0

--- a/solution.py
+++ b/solution.py
@@ -150,7 +150,8 @@
         lax.psum_scatter(grad_vals, "head", scatter_dimension=0, tiled=True),
     )
     grad_qweight = lax.psum(jnp.stack(weight_grads, axis=0), "ctx")
-    grad_kweight = lax.psum(grad_kweight, ("ctx", "head"))
+    partial = lax.psum(grad_kweight, "head")
+    grad_kweight = lax.psum(partial, "ctx")
     return (
         jnp.concatenate(query_grads, axis=1),
         grad_keys,

time: 1220 us -> 978 us (0.80)
  waiting for transfers between devices: 740 us -> 494 us
    psum x1, waiting for transfers between devices: 440 us -> 69.6 us  [on_device(): partial = lax.psum(grad_kweight, 'head')]
    psum x1, waiting for transfers between devices: 138 us -> 260 us  [on_device(): grad_qweight = lax.psum(jnp.stack(weight_grads, axis=0), 'ctx')]
  transfers between devices with their start and end apart: 6 -> 6, of which waited for: 6 -> 6; matrix products, arithmetic and copies ran while one was open for 14% -> 6% of each run, Pallas kernels for 0% -> 0%
where the time goes in v1:
time: 978 us; the launch traced here: 970 us
  waiting for transfers between devices  494 us (51%)
  blocking collectives  168 us (17%)
  other arithmetic  133 us (14%)
  local copies, waits for them, and re-layouts  116 us (12%)
  matrix products  40.2 us (4%)
  between operations  14.6 us (1%)
    psum x1, waiting for transfers between devices, on_device(): grad_qweight = lax.psum(jnp.stack(weight_grads, axis=0), 'ctx')  260 us
    all_gather x2, blocking collectives, entering(): pieces = jax.tree.map(lambda part: lax.all_gather(part, axis), value)  168 us
    select_n x252, other arithmetic, turn(): jnp.where(position < mine, new, old)  121 us
    all_gather x2, waiting for transfers between devices, entering(): pieces = jax.tree.map(lambda part: lax.all_gather(part, axis), value)  90.9 us
    dynamic_slice x126, local copies, waits for them, and re-layouts, turn(): longer = join(total, jax.tree.map(lambda part: part[position], pieces))  89 us
    psum x1, waiting for transfers between devices, on_device(): partial = lax.psum(grad_kweight, 'head')  69.6 us
    reduce_scatter x1, waiting for transfers between devices, on_device(): lax.psum_scatter(grad_key_part, 'head', scatter_dimension=0, tiled=True)  40.6 us
    reduce_scatter x1, waiting for transfers between devices, on_device(): lax.psum_scatter(grad_vals, 'head', scatter_dimension=0, tiled=True)  33.2 us
  transfers between devices with their start and end apart: 6, of which 6 were waited for; matrix products, arithmetic and copies ran while one was open for 6% of the time, Pallas kernels for 0%

profile of v1, /device:TPU:2, one launch (start us, length us, event | category | flops | bytes accessed | tf_op | source)
XLA Modules:
  0.0 969.5 jit_solution(3737522410225893496)
XLA Ops:
  9.8 2.1 fusion.103
  14.9 87.9 %all-gather.4 = f32[64,1,256]{2,1,0:T(1,128)S(1)} all-gather(f32[1,1,256]{2,1,0:T(1,128)S(1)} %bitcast.226), channel_id=3, replica_groups=mesh['ctx'=64,'head'=8] {'ctx'}, dimensions={0}, use_global_device_ids=true | all-gather | bytes 66560 | tf_op jit(solution)/shard_map/all_gather | solution.py:9
  106.6 1.8 fusion.102
  108.4 1.8 fusion.104
  110.2 62.4 %all-gather.9.cloned.1.call-done = f32[16384,128]{1,0:T(8,128)} async-done(((f32[256,128]{1,0:T(8,128)}), f32[16384,128]{1,0:T(8,128)}) %all-gather.9.cloned.1.call-update) | async-done | bytes 8388624 | tf_op jit(solution)/shard_map/all_gather | solution.py:9
  172.6 106.3 %while.32 = (s32[]{:T(128)}, f32[256,128]{1,0:T(8,128)S(1)}, f32[256]{0:T(256)S(1)}, s32[]{:T(128)}, f32[64,256,128]{2,1,0:T(8,128)}, /*index=5*/f32[64,256]{1,0:T(8,128)}, s32[]{:T(128)}, s32[]{:T(128)}) while((s32[]{:T(128)}, f32[256,128]{1,0:T(8,128)S(1)}, f32[256]{0:T(256)S(1)}, s32[]{:T(128)}, f32[64,256,128]{2,1,0:T(8,128)}, ...), condition=%wide.region_15.16_spmd.clone, body=%wide.region_14.15_spmd.clone.sunk | while | flops 99076 | bytes 398459 | solution.py:21
  280.5 2.1 fusion.105
  287.9 1.6 fusion.15
  290.7 80.2 %all-gather.5 = f32[64,1,256]{2,1,0:T(1,128)S(1)} all-gather(f32[1,1,256]{2,1,0:T(1,128)S(1)} %bitcast.225), channel_id=5, replica_groups=mesh['ctx'=64,'head'=8] {'ctx'}, dimensions={0}, use_global_device_ids=true | all-gather | bytes 66560 | tf_op jit(solution)/shard_map/all_gather | solution.py:9
  374.8 1.8 copy.214
  376.6 1.8 copy.215
  390.7 2.0 copy.209
  392.7 1.8 copy.213
  401.7 1.7 fusion.93
  404.4 1.6 fusion.7
  406.1 28.5 %all-gather.11.cloned.1.call-done = f32[16384,128]{1,0:T(8,128)} async-done(((f32[256,128]{1,0:T(8,128)}), f32[16384,128]{1,0:T(8,128)}) %all-gather.11.cloned.1.call-update) | async-done | bytes 8388624 | tf_op jit(solution)/shard_map/all_gather | solution.py:9
  434.6 7.7 rev.6
  442.2 106.4 %while.33 = (s32[]{:T(128)}, f32[256,128]{1,0:T(8,128)S(1)}, f32[256]{0:T(256)S(1)}, s32[]{:T(128)}, f32[64,256,128]{2,1,0:T(8,128)}, /*index=5*/f32[64,256]{1,0:T(8,128)}, s32[]{:T(128)}, s32[]{:T(128)}) while((s32[]{:T(128)}, f32[256,128]{1,0:T(8,128)S(1)}, f32[256]{0:T(256)S(1)}, s32[]{:T(128)}, f32[64,256,128]{2,1,0:T(8,128)}, ...), condition=%wide.region_33.34_spmd.clone, body=%wide.region_32.33_spmd.clone.sunk | while | flops 99076 | bytes 398459 | solution.py:21
  551.2 69.6 %all-reduce.4.cloned.1.call-done = f32[128,128]{0,1:T(8,128)} async-done(((f32[128,128]{0,1:T(8,128)}), f32[128,128]{0,1:T(8,128)}) %all-reduce.4.cloned.1.call-update) | async-done | bytes 65552 | tf_op jit(solution)/shard_map/psum | solution.py:153
  621.1 1.7 convolution_add_fusion.5
  626.1 259.6 %all-reduce.6.cloned.1.call-done = (f32[2,128,128]{1,2,0:T(8,128)}, f32[128,128]{0,1:T(8,128)}) async-done(((f32[2,128,128]{1,2,0:T(8,128)}, f32[128,128]{0,1:T(8,128)}), (f32[2,128,128]{1,2,0:T(8,128)}, f32[128,128]{0,1:T(8,128)})) %all-reduce.6.cloned.1.call-update) | async-done | bytes 196624 | tf_op jit(solution)/shard_map/psum | solution.py:152
  885.7 1.7 copy.181
  888.9 33.2 %reduce-scatter.5.cloned.1.call-done = f32[64,128]{1,0:T(8,128)} async-done(((f32[512,128]{1,0:T(8,128)}), f32[64,128]{1,0:T(8,128)}) %reduce-scatter.5.cloned.1.call-update) | async-done | bytes 32784 | tf_op jit(solution)/shard_map/reduce_scatter | solution.py:150
  922.1 40.6 %reduce-scatter.3.cloned.1.call-done = f32[64,128]{1,0:T(8,128)} async-done(((f32[512,128]{1,0:T(8,128)}), f32[64,128]{1,0:T(8,128)}) %reduce-scatter.3.cloned.1.call-update) | async-done | bytes 32784 | tf_op jit(solution)/shard_map/reduce_scatter | solution.py:149
  (497 shorter events, 258.7 us)
Async XLA Ops:
  7.2 2.6 copy-start
  7.2 98.1 %copy-start.12 = (f32[2,128,128]{2,1,0:T(8,128)S(1)}, f32[2,128,128]{2,1,0:T(8,128)}, u32[]{:S(2)}) copy-start(f32[2,128,128]{2,1,0:T(8,128)} %param.18) | copy-start | bytes 393220
  7.2 98.1 %copy-start.4 = (f32[512,256]{1,0:T(8,128)S(1)}, f32[512,256]{1,0:T(8,128)}, u32[]{:S(2)}) copy-start(f32[512,256]{1,0:T(8,128)} %param.12) | copy-start | bytes 1572868
  7.2 165.4 %all-gather.9.cloned.1.call-start = ((), (), s32[]{:S(2)}) async-start(), calls=%async_computation.5 | async-start | bytes 8519680 | tf_op jit(solution)/shard_map/all_gather | solution.py:9
  11.9 422.6 %all-gather.11.cloned.1.call-start = ((), (), s32[]{:S(2)}) async-start(), calls=%async_computation.6 | async-start | bytes 8519680 | tf_op jit(solution)/shard_map/all_gather | solution.py:9
  105.1 174.8 %copy-start.8 = (f32[4,128,128]{1,2,0:T(8,128)S(1)}, f32[4,128,128]{1,2,0:T(8,128)}, u32[]{:S(2)}) copy-start(f32[4,128,128]{1,2,0:T(8,128)} %copy.142) | copy-start | bytes 786436
  105.3 173.6 %copy-start.10 = (f32[128,128]{0,1:T(8,128)}, f32[128,128]{0,1:T(8,128)S(1)}, u32[]{:S(2)}) copy-start(f32[128,128]{0,1:T(8,128)S(1)} %fusion.88) | copy-start | bytes 196612
  279.0 92.5 %copy-start.11 = (f32[128,128]{0,1:T(8,128)S(1)}, f32[128,128]{0,1:T(8,128)}, u32[]{:S(2)}) copy-start(f32[128,128]{0,1:T(8,128)} %copy-done.10) | copy-start | bytes 196612
  282.6 338.2 %all-reduce.4.cloned.1.call-start = ((), (), s32[]{:S(2)}) async-start(), calls=%async_computation.4 | async-start | bytes 131072 | tf_op jit(solution)/shard_map/psum | solution.py:153
  290.6 90.5 %copy-start.15 = (f32[256]{0:T(256)}, f32[256]{0:T(256)S(1)}, u32[]{:S(2)}) copy-start(f32[256]{0:T(256)S(1)} %get-tuple-element.331) | copy-start | bytes 3076
  372.0 0.7 copy-start.6
  379.8 0.7 copy-start.7
  382.8 11.8 %copy-start.3 = (f32[512,128]{0,1:T(8,128)S(1)}, f32[512,128]{0,1:T(8,128)}, u32[]{:S(2)}) copy-start(f32[512,128]{0,1:T(8,128)} %copy.214) | copy-start | bytes 786436
  396.6 7.8 copy-start.1
  434.6 114.0 %copy-start.5 = (f32[512,256]{0,1:T(8,128)S(1)}, f32[512,256]{0,1:T(8,128)}, u32[]{:S(2)}) copy-start(f32[512,256]{0,1:T(8,128)} %copy.209) | copy-start | bytes 1572868
  434.6 114.9 %copy-start.9 = (f32[512,128]{1,0:T(8,128)S(1)}, f32[512,128]{1,0:T(8,128)}, u32[]{:S(2)}) copy-start(f32[512,128]{1,0:T(8,128)} %param.13) | copy-start | bytes 786436
  442.2 180.7 %copy-start.14 = (f32[128,128]{1,0:T(8,128)S(1)}, f32[128,128]{1,0:T(8,128)}, u32[]{:S(2)}) copy-start(f32[128,128]{1,0:T(8,128)} %param.19) | copy-start | bytes 196612
  442.2 182.0 %copy-start.2 = (f32[512,128]{0,1:T(8,128)S(1)}, f32[512,128]{0,1:T(8,128)}, u32[]{:S(2)}) copy-start(f32[512,128]{0,1:T(8,128)} %copy-done.1) | copy-start | bytes 786436
  442.2 182.0 %copy-start.13 = (f32[2,128,128]{2,1,0:T(8,128)S(1)}, f32[2,128,128]{2,1,0:T(8,128)}, u32[]{:S(2)}) copy-start(f32[2,128,128]{2,1,0:T(8,128)} %param.18) | copy-start | bytes 393220
  550.5 335.2 %all-reduce.6.cloned.1.call-start = ((), (), s32[]{:S(2)}) async-start(), calls=%async_computation.7 | async-start | bytes 393216 | tf_op jit(solution)/shard_map/psum | solution.py:152
  620.9 301.2 %reduce-scatter.5.cloned.1.call-start = ((), (), s32[]{:S(2)}) async-start(), calls=%async_computation.3 | async-start | bytes 294912 | tf_op jit(solution)/shard_map/reduce_scatter | solution.py:150
  622.9 339.8 %reduce-scatter.3.cloned.1.call-start = ((), (), s32[]{:S(2)}) async-start(), calls=%async_computation.2 | async-start | bytes 294912 | tf_op jit(solution)/shard_map/reduce_scatter | solution.py:149
Sparse Core Ops, SparseCore 0:
  12.0 160.5 all-gather.8
  282.7 151.7 all-gather.10
  550.6 70.1 all-reduce.3
  625.2 260.4 all-reduce.5
  888.9 33.1 reduce-scatter.4
  925.5 37.0 reduce-scatter.2
